TPU v7x, 512 devices: a whole 4x4x16 slice. The times are simulated.
512 devices in a mesh: dp: 4 (over x), expert: 128 (over z, y, core).
Axes of the slice: x: 4, y: 4, z: 16, core: 2. Of those that a mesh axis runs over, the one named last changes fastest.
Arguments:
- tokens: bfloat16 [8192, 2048], P(('dp', 'expert')), may hold values from -6 to 6
- cotangent: bfloat16 [8192, 2048], P(('dp', 'expert')), may hold values from -6 to 6
- expert_ids: int32 [8192, 8], P(('dp', 'expert')), may hold values from 0 to 127, all different within a row; in each aligned block of 16 rows (0 to 15, 16 to 31, ...) at most 2 rows name the same one
- gate_values: float32 [8192, 8], P(('dp', 'expert')), may hold values from 0.05 to 0.5
- gate_weight: bfloat16 [128, 2048, 384], P('expert', 'dp'), may hold values from -0.125 to 0.125
- up_weight: bfloat16 [128, 2048, 384], P('expert', 'dp'), may hold values from -0.125 to 0.125
- down_weight: bfloat16 [128, 2048, 384], P('expert', 'dp'), may hold values from -0.3125 to 0.3125
Outputs:
- mixed: bfloat16 [8192, 2048], P(('dp', 'expert'))
- input_grad: bfloat16 [8192, 2048], P(('dp', 'expert'))
- gate_grad: float32 [8192, 8], P(('dp', 'expert'))
- gate_weight_grad: float32 [128, 2048, 384], P('expert', 'dp')
- up_weight_grad: float32 [128, 2048, 384], P('expert', 'dp')
Inputs may be any that keep to these rules, and one draw needn't show every extreme that they name: `expert_ids`: each row names 8 different experts. Among the 16 rows of one device no expert is named more than 2 times.
All inputs are finite; a program needn't handle non-finite values.
Results may differ from a plain program's by a relative error of at most 0.012.
Values may be sent and summed in bfloat16 or wider, within the bound.
A program may use at most 64 MiB of HBM per device.

v0:
```python
import jax
import jax.numpy as jnp
from jax import lax
from jax.sharding import PartitionSpec as P


def body(tokens, cotangent, expert_ids, gate_values, gate_weight, up_weight, down_weight):
    tok_rows = tokens.shape[0]
    feature_width = tokens.shape[1]
    top_count = expert_ids.shape[1]
    experts = lax.axis_size("expert")
    routed = tok_rows * top_count
    capacity = min(tok_rows, max(2, (routed + experts - 1) // experts + 1))
    flat_ids = expert_ids.reshape(routed)
    onehot = (flat_ids[:, None] == jnp.arange(experts, dtype=jnp.int32)[None, :]).astype(jnp.int32)
    earlier = jnp.cumsum(onehot, axis=0) - onehot
    slot_rank = jnp.sum(earlier * onehot, axis=1)
    target = flat_ids * capacity + slot_rank
    owner_row = jnp.arange(routed, dtype=jnp.int32) // top_count
    gate_flat = gate_values.reshape(routed)
    picked = tokens[owner_row]
    scaled = (gate_flat[:, None] * cotangent[owner_row].astype(jnp.float32)).astype(jnp.bfloat16)
    slot_count = experts * capacity
    send_rows = jnp.zeros((slot_count, feature_width), jnp.bfloat16).at[target].set(picked)
    send_rows = send_rows.reshape(experts, capacity, feature_width)
    send_grads = jnp.zeros((slot_count, feature_width), jnp.bfloat16).at[target].set(scaled)
    send_grads = send_grads.reshape(experts, capacity, feature_width)
    gate_full, up_full, down_full = (
        lax.all_gather(gate_weight, "dp", axis=1, tiled=True),
        lax.all_gather(up_weight, "dp", axis=1, tiled=True),
        lax.all_gather(down_weight, "dp", axis=1, tiled=True),
    )
    gate_mat = gate_full[0]
    up_mat = up_full[0]
    arrived = lax.all_to_all(send_rows, "expert", split_axis=0, concat_axis=0, tiled=True)
    rows = arrived.reshape(slot_count, feature_width)
    hidden_gate = jnp.dot(rows, gate_mat, preferred_element_type=jnp.float32)
    hidden_up = jnp.dot(rows, up_mat, preferred_element_type=jnp.float32)
    down_mat = down_full[0]
    sigma = jax.nn.sigmoid(hidden_gate)
    active = (hidden_gate * sigma * hidden_up).astype(jnp.bfloat16)
    contract_last = (((1,), (1,)), ((), ()))
    outputs = lax.dot_general(
        active, down_mat, contract_last, preferred_element_type=jnp.float32
    ).astype(jnp.bfloat16)
    outputs = outputs.reshape(experts, capacity, feature_width)
    returned = lax.all_to_all(outputs, "expert", split_axis=0, concat_axis=0, tiled=True)
    arrived_grads = lax.all_to_all(send_grads, "expert", split_axis=0, concat_axis=0, tiled=True)
    grad_rows = arrived_grads.reshape(slot_count, feature_width)
    grad_active = jnp.dot(grad_rows, down_mat, preferred_element_type=jnp.float32)
    grad_up = (grad_active * hidden_gate * sigma).astype(jnp.bfloat16)
    grad_gate = (grad_active * hidden_up * sigma * (1.0 + hidden_gate * (1.0 - sigma))).astype(
        jnp.bfloat16
    )
    input_rows = lax.dot_general(
        grad_gate, gate_mat, contract_last, preferred_element_type=jnp.float32
    )
    input_rows = input_rows + lax.dot_general(
        grad_up, up_mat, contract_last, preferred_element_type=jnp.float32
    )
    input_rows = input_rows.astype(jnp.bfloat16).reshape(experts, capacity, feature_width)
    returned_grads = lax.all_to_all(input_rows, "expert", split_axis=0, concat_axis=0, tiled=True)
    contract_rows = (((0,), (0,)), ((), ()))
    gate_part = lax.dot_general(rows, grad_gate, contract_rows, preferred_element_type=jnp.float32)
    up_part = lax.dot_general(rows, grad_up, contract_rows, preferred_element_type=jnp.float32)
    gate_weight_grad, up_weight_grad = (
        lax.psum_scatter(
            gate_part[None].astype(jnp.bfloat16), "dp", scatter_dimension=1, tiled=True
        ).astype(jnp.float32),
        lax.psum_scatter(
            up_part[None].astype(jnp.bfloat16), "dp", scatter_dimension=1, tiled=True
        ).astype(jnp.float32),
    )
    back_rows = returned.reshape(slot_count, feature_width)[target].astype(jnp.float32)
    back_rows = back_rows.reshape(tok_rows, top_count, feature_width)
    back_grads = returned_grads.reshape(slot_count, feature_width)[target].astype(jnp.float32)
    back_grads = back_grads.reshape(tok_rows, top_count, feature_width)
    weights_here = gate_flat.reshape(tok_rows, top_count)
    mixed = jnp.sum(weights_here[:, :, None] * back_rows, axis=1).astype(jnp.bfloat16)
    gate_grad = jnp.sum(back_rows * cotangent.astype(jnp.float32)[:, None, :], axis=2)
    input_grad = jnp.sum(back_grads, axis=1).astype(jnp.bfloat16)
    return (mixed, input_grad, gate_grad, gate_weight_grad, up_weight_grad)


def solution(mesh):
    placed = (
        P(("dp", "expert"), None),
        P(("dp", "expert"), None),
        P(("dp", "expert"), None),
        P(("dp", "expert"), None),
        P("expert", "dp", None),
        P("expert", "dp", None),
        P("expert", "dp", None),
    )
    return jax.shard_map(
        body,
        mesh=mesh,
        in_specs=placed,
        out_specs=(
            P(("dp", "expert"), None),
            P(("dp", "expert"), None),
            P(("dp", "expert"), None),
            P("expert", "dp", None),
            P("expert", "dp", None),
        ),
        check_vma=False,
    )
```

profile of v0, /device:TPU:33, one launch (start us, length us, event | category | flops | bytes accessed | tf_op | source)
XLA Modules:
  0.0 292.1 jit_solution(706173469473217055)
XLA Ops:
  9.4 3.4 %scatter_custom_fusion = bf16[256,2048]{1,0:T(8,128)(2,1)S(1)} fusion(s32[128]{0:T(128)S(1)} %fusion.24, bf16[16,2048]{1,0:T(8,128)(2,1)S(1)} %copy-done, s32[1024]{0:T(1024)S(1)} %pad_clamp_fusion.1, bf16[]{:T(256)} %constant.26.clone.1), kind=kCustom, calls=%fused_computation.30 | custom fusion | bytes 1048578 | tf_op jit(solution)/shard_map/scatter | solution.py:24
  14.3 19.6 %all-to-all-start = ((bf16[128,2,2048]{2,1,0:T(2,128)(2,1)}), bf16[128,2,2048]{2,1,0:T(2,128)(2,1)S(1)}, u32[]{:S(2)}, u32[]{:S(2)}) async-start(bf16[128,2,2048]{2,1,0:T(2,128)(2,1)} %reshape.128), calls=%async_computation | async-start | bytes 2097152 | tf_op jit(solution)/shard_map/all_to_all | solution.py:35
  35.6 3.4 %scatter_custom_fusion.1 = bf16[256,2048]{1,0:T(8,128)(2,1)S(1)} fusion(s32[128]{0:T(128)S(1)} %fusion.24, f32[128]{0:T(128)S(1)} %mul.81, bf16[]{:T(256)} %constant.26.clone.1, bf16[16,2048]{1,0:T(8,128)(2,1)S(1)} %copy-done.3, s32[1024]{0:T(1024)S(1)} %pad_clamp_fusion.1), kind=kCustom, calls=%fused_computation.28 | custom fusion | flops 786432 | bytes 1118722 | tf_op jit(solution)/shard_map/scatter | solution.py:26
  39.0 1.5 reshape.132
  40.5 49.0 %all-to-all-done = bf16[128,2,2048]{2,1,0:T(2,128)(2,1)S(1)} async-done(((bf16[128,2,2048]{2,1,0:T(2,128)(2,1)}), bf16[128,2,2048]{2,1,0:T(2,128)(2,1)S(1)}, u32[]{:S(2)}, u32[]{:S(2)}) %all-to-all-start) | async-done | bytes 1048608 | tf_op jit(solution)/shard_map/all_to_all | solution.py:35
  89.5 6.4 %all-to-all-start.2 = ((bf16[128,2,2048]{2,1,0:T(2,128)(2,1)}), bf16[128,2,2048]{2,1,0:T(2,128)(2,1)S(1)}, u32[]{:S(2)}, u32[]{:S(2)}) async-start(bf16[128,2,2048]{2,1,0:T(2,128)(2,1)} %reshape.132), calls=%async_computation.2 | async-start | bytes 2097152 | tf_op jit(solution)/shard_map/all_to_all | solution.py:48
  97.2 2.9 fusion.7
  100.0 8.2 %all-gather.4.cloned.1.call-done = bf16[1,2048,384]{2,1,0:T(8,128)(2,1)} async-done(((bf16[1,512,384]{2,1,0:T(8,128)(2,1)}), bf16[1,2048,384]{2,1,0:T(8,128)(2,1)}) %all-gather.4.cloned.1.call-update) | async-done | bytes 1572880 | tf_op jit(solution)/shard_map/all_gather | solution.py:29
  108.2 2.9 fusion.11
  111.1 33.6 %all-gather.8.cloned.1.call-done = bf16[1,2048,384]{2,1,0:T(8,128)(2,1)} async-done(((bf16[1,512,384]{2,1,0:T(8,128)(2,1)}), bf16[1,2048,384]{2,1,0:T(8,128)(2,1)}) %all-gather.8.cloned.1.call-update) | async-done | bytes 1572880 | tf_op jit(solution)/shard_map/all_gather | solution.py:31
  144.7 2.4 convolution_convert_fusion.2
  147.1 1.5 reshape.130
  148.6 2.9 %all-to-all-done.2 = bf16[128,2,2048]{2,1,0:T(2,128)(2,1)S(1)} async-done(((bf16[128,2,2048]{2,1,0:T(2,128)(2,1)}), bf16[128,2,2048]{2,1,0:T(2,128)(2,1)S(1)}, u32[]{:S(2)}, u32[]{:S(2)}) %all-to-all-start.2) | async-done | bytes 1048608 | tf_op jit(solution)/shard_map/all_to_all | solution.py:48
  151.6 14.3 %all-to-all-start.1 = ((bf16[128,2,2048]{2,1,0:T(2,128)(2,1)}), bf16[128,2,2048]{2,1,0:T(2,128)(2,1)}, u32[]{:S(2)}, u32[]{:S(2)}) async-start(bf16[128,2,2048]{2,1,0:T(2,128)(2,1)} %reshape.130), calls=%async_computation.1 | async-start | bytes 2097152 | tf_op jit(solution)/shard_map/all_to_all | solution.py:47
  166.4 2.4 multiply_convert_fusion.2
  168.7 1.9 fusion
  174.4 46.8 %all-to-all-done.1 = bf16[128,2,2048]{2,1,0:T(2,128)(2,1)} async-done(((bf16[128,2,2048]{2,1,0:T(2,128)(2,1)}), bf16[128,2,2048]{2,1,0:T(2,128)(2,1)}, u32[]{:S(2)}, u32[]{:S(2)}) %all-to-all-start.1) | async-done | bytes 1048608 | tf_op jit(solution)/shard_map/all_to_all | solution.py:47
  221.1 6.4 %all-to-all-start.3 = ((bf16[128,2,2048]{2,1,0:T(2,128)(2,1)}), bf16[128,2,2048]{2,1,0:T(2,128)(2,1)S(1)}, u32[]{:S(2)}, u32[]{:S(2)}) async-start(bf16[128,2,2048]{2,1,0:T(2,128)(2,1)} %reshape.134), calls=%async_computation.3 | async-start | bytes 2097152 | tf_op jit(solution)/shard_map/all_to_all | solution.py:62
  227.8 1.9 fusion.1
  229.8 1.9 convert_element_type.76
  231.8 31.1 %reduce-scatter.5.cloned.1.call-done = bf16[1,512,384]{2,1,0:T(8,128)(2,1)} async-done(((bf16[1,2048,384]{2,1,0:T(8,128)(2,1)}), bf16[1,512,384]{2,1,0:T(8,128)(2,1)}) %reduce-scatter.5.cloned.1.call-update) | async-done | bytes 393232 | tf_op jit(solution)/shard_map/reduce_scatter | solution.py:70
  262.8 1.9 convert_element_type.79
  267.2 1.7 fusion.14
  269.5 13.7 %all-to-all-done.3 = bf16[128,2,2048]{2,1,0:T(2,128)(2,1)S(1)} async-done(((bf16[128,2,2048]{2,1,0:T(2,128)(2,1)}), bf16[128,2,2048]{2,1,0:T(2,128)(2,1)S(1)}, u32[]{:S(2)}, u32[]{:S(2)}) %all-to-all-start.3) | async-done | bytes 1048608 | tf_op jit(solution)/shard_map/all_to_all | solution.py:62
  (49 shorter events, 16.4 us)
Async XLA Ops:
  7.2 2.2 copy-start
  14.3 21.1 %copy-start.4 = (f32[16,8]{0,1:T(8,128)S(1)}, f32[16,8]{0,1:T(8,128)}, u32[]{:S(2)}) copy-start(f32[16,8]{0,1:T(8,128)} %param.10) | copy-start | bytes 1540
  14.3 21.3 %copy-start.3 = (bf16[16,2048]{1,0:T(8,128)(2,1)S(1)}, bf16[16,2048]{1,0:T(8,128)(2,1)}, u32[]{:S(2)}) copy-start(bf16[16,2048]{1,0:T(8,128)(2,1)} %param.8) | copy-start | bytes 196612
  14.3 75.2 %all-to-all-start = ((bf16[128,2,2048]{2,1,0:T(2,128)(2,1)}), bf16[128,2,2048]{2,1,0:T(2,128)(2,1)S(1)}, u32[]{:S(2)}, u32[]{:S(2)}) async-start(bf16[128,2,2048]{2,1,0:T(2,128)(2,1)} %reshape.128), calls=%async_computation | async-start | bytes 2097152 | tf_op jit(solution)/shard_map/all_to_all | solution.py:35
  33.9 63.3 %all-gather.6.cloned.1.call-start = ((), (), s32[]{:S(2)}) async-start(), calls=%async_computation.7 | async-start | bytes 1966080 | tf_op jit(solution)/shard_map/all_gather | solution.py:30
  34.6 73.6 %all-gather.4.cloned.1.call-start = ((), (), s32[]{:S(2)}) async-start(), calls=%async_computation.6 | async-start | bytes 1966080 | tf_op jit(solution)/shard_map/all_gather | solution.py:29
  89.5 62.1 %all-to-all-start.2 = ((bf16[128,2,2048]{2,1,0:T(2,128)(2,1)}), bf16[128,2,2048]{2,1,0:T(2,128)(2,1)S(1)}, u32[]{:S(2)}, u32[]{:S(2)}) async-start(bf16[128,2,2048]{2,1,0:T(2,128)(2,1)} %reshape.132), calls=%async_computation.2 | async-start | bytes 2097152 | tf_op jit(solution)/shard_map/all_to_all | solution.py:48
  96.0 48.7 %all-gather.8.cloned.1.call-start = ((), (), s32[]{:S(2)}) async-start(), calls=%async_computation.8 | async-start | bytes 1966080 | tf_op jit(solution)/shard_map/all_gather | solution.py:31
  151.6 69.6 %all-to-all-start.1 = ((bf16[128,2,2048]{2,1,0:T(2,128)(2,1)}), bf16[128,2,2048]{2,1,0:T(2,128)(2,1)}, u32[]{:S(2)}, u32[]{:S(2)}) async-start(bf16[128,2,2048]{2,1,0:T(2,128)(2,1)} %reshape.130), calls=%async_computation.1 | async-start | bytes 2097152 | tf_op jit(solution)/shard_map/all_to_all | solution.py:47
  165.9 64.0 %reduce-scatter.3.cloned.1.call-start = ((), (), s32[]{:S(2)}) async-start(), calls=%async_computation.9 | async-start | bytes 1966080 | tf_op jit(solution)/shard_map/reduce_scatter | solution.py:67
  168.7 1.9 copy-start.2
  170.7 1.4 copy-start.1
  221.1 62.1 %all-to-all-start.3 = ((bf16[128,2,2048]{2,1,0:T(2,128)(2,1)}), bf16[128,2,2048]{2,1,0:T(2,128)(2,1)S(1)}, u32[]{:S(2)}, u32[]{:S(2)}) async-start(bf16[128,2,2048]{2,1,0:T(2,128)(2,1)} %reshape.134), calls=%async_computation.3 | async-start | bytes 2097152 | tf_op jit(solution)/shard_map/all_to_all | solution.py:62
  227.6 35.3 %reduce-scatter.5.cloned.1.call-start = ((), (), s32[]{:S(2)}) async-start(), calls=%async_computation.10 | async-start | bytes 1966080 | tf_op jit(solution)/shard_map/reduce_scatter | solution.py:70
Sparse Core Ops, SparseCore 0:
  36.8 34.8 all-gather.5
  73.9 34.3 all-gather.3
  110.3 34.3 all-gather.7
  170.8 31.8 reduce-scatter.2
  230.9 31.8 reduce-scatter.4
where the time goes:
time: 293 us; the launch traced here: 292 us
  waiting for transfers between devices  187 us (64%)
  starting transfers between devices  47.4 us (16%)
  local copies, waits for them, and re-layouts  16.5 us (6%)
  matrix products  15.8 us (5%)
  between operations  14 us (5%)
  other arithmetic  11.1 us (4%)
    all_to_all x1, waiting for transfers between devices, body(): lax.all_to_all(send_rows, 'expert', split_axis=0, concat_axis=0, tiled=True)  49 us
    all_to_all x1, waiting for transfers between devices, body(): lax.all_to_all(outputs, 'expert', split_axis=0, concat_axis=0, tiled=True)  46.8 us
    all_gather x1, waiting for transfers between devices, body(): lax.all_gather(down_weight, 'dp', axis=1, tiled=True)  33.6 us
    reduce_scatter x1, waiting for transfers between devices, body(): lax.psum_scatter(up_part[None].astype(jnp.bfloat16), 'dp', scatter_dimens...  31.1 us
    all_to_all x1, starting transfers between devices, body(): lax.all_to_all(send_rows, 'expert', split_axis=0, concat_axis=0, tiled=True)  19.6 us
    all_to_all x1, starting transfers between devices, body(): lax.all_to_all(outputs, 'expert', split_axis=0, concat_axis=0, tiled=True)  14.3 us
    all_to_all x1, waiting for transfers between devices, body(): lax.all_to_all(input_rows, 'expert', split_axis=0, concat_axis=0, tiled=T...  13.7 us
    all_gather x1, waiting for transfers between devices, body(): lax.all_gather(gate_weight, 'dp', axis=1, tiled=True)  8.2 us
  transfers between devices with their start and end apart: 9, of which 7 were waited for; matrix products, arithmetic and copies ran while one was open for 11% of the time, Pallas kernels for 0%

commit v1 on v0

--- a/solution.py
+++ b/solution.py
@@ -2,6 +2,11 @@
 import jax.numpy as jnp
 from jax import lax
 from jax.sharding import PartitionSpec as P
+
+
+def swapped_in(x, axis, along):
+    stack = jnp.stack([x] * lax.axis_size(axis))
+    return jnp.concatenate(lax.all_to_all(stack, axis, 0, 0), axis=along)
 
 
 def body(tokens, cotangent, expert_ids, gate_values, gate_weight, up_weight, down_weight):
@@ -28,7 +33,7 @@
     gate_full, up_full, down_full = (
         lax.all_gather(gate_weight, "dp", axis=1, tiled=True),
         lax.all_gather(up_weight, "dp", axis=1, tiled=True),
-        lax.all_gather(down_weight, "dp", axis=1, tiled=True),
+        swapped_in(down_weight, "dp", 1),
     )
     gate_mat = gate_full[0]
     up_mat = up_full[0]

time: 293 us -> 309 us (1.055)
  waiting for transfers between devices: 187 us -> 205 us
  local copies, waits for them, and re-layouts: 16.5 us -> 20.1 us
    all_gather x1 -> x0, waiting for transfers between devices: 33.6 us -> none  [body(): lax.all_gather(down_weight, 'dp', axis=1, tiled=True)]
    all_gather x1, waiting for transfers between devices: 8.2 us -> 31.9 us  [body(): lax.all_gather(gate_weight, 'dp', axis=1, tiled=True)]
    all_to_all x0 -> x1, waiting for transfers between devices: none -> 14.1 us  [swapped_in(): return jnp.concatenate(lax.all_to_all(stack, axis, 0, 0), axis=along)]
    all_to_all x1, waiting for transfers between devices: 2.94 us -> 14.3 us  [body(): lax.all_to_all(send_grads, 'expert', split_axis=0, concat_axis=0, tiled=T...]
    all_to_all x1, starting transfers between devices: 14.3 us -> 6.9 us  [body(): lax.all_to_all(outputs, 'expert', split_axis=0, concat_axis=0, tiled=True)]
    all_to_all x0 -> x1, starting transfers between devices: none -> 4.14 us  [swapped_in(): return jnp.concatenate(lax.all_to_all(stack, axis, 0, 0), axis=along)]
where the time goes in v1:
time: 309 us; the launch traced here: 308 us
  waiting for transfers between devices  205 us (66%)
  starting transfers between devices  45.2 us (15%)
  local copies, waits for them, and re-layouts  20.1 us (7%)
  between operations  14 us (5%)
  matrix products  13.5 us (4%)
  other arithmetic  10.4 us (3%)
    all_to_all x1, waiting for transfers between devices, body(): lax.all_to_all(send_rows, 'expert', split_axis=0, concat_axis=0, tiled=True)  49.7 us
    all_to_all x1, waiting for transfers between devices, body(): lax.all_to_all(outputs, 'expert', split_axis=0, concat_axis=0, tiled=True)  46.8 us
    all_gather x1, waiting for transfers between devices, body(): lax.all_gather(gate_weight, 'dp', axis=1, tiled=True)  31.9 us
    reduce_scatter x1, waiting for transfers between devices, body(): lax.psum_scatter(up_part[None].astype(jnp.bfloat16), 'dp', scatter_dimens...  30.4 us
    all_to_all x1, starting transfers between devices, body(): lax.all_to_all(send_rows, 'expert', split_axis=0, concat_axis=0, tiled=True)  20.7 us
    all_to_all x1, waiting for transfers between devices, body(): lax.all_to_all(input_rows, 'expert', split_axis=0, concat_axis=0, tiled=T...  16.7 us
    all_to_all x1, waiting for transfers between devices, body(): lax.all_to_all(send_grads, 'expert', split_axis=0, concat_axis=0, tiled=T...  14.3 us
    all_to_all x1, waiting for transfers between devices, swapped_in(): return jnp.concatenate(lax.all_to_all(stack, axis, 0, 0), axis=along)  14.1 us
  transfers between devices with their start and end apart: 9, of which 7 were waited for; matrix products, arithmetic and copies ran while one was open for 11% of the time, Pallas kernels for 0%

profile of v1, /device:TPU:33, one launch (start us, length us, event | category | flops | bytes accessed | tf_op | source)
XLA Modules:
  0.0 308.4 jit_solution(16272077377600392017)
XLA Ops:
  7.2 2.3 stack.2
  9.5 4.1 %all-to-all-start.1 = ((bf16[4,1,512,384]{3,2,1,0:T(8,128)(2,1)}), bf16[4,1,512,384]{3,2,1,0:T(8,128)(2,1)S(1)}, u32[]{:S(2)}, u32[]{:S(2)}) async-start(bf16[4,1,512,384]{3,2,1,0:T(8,128)(2,1)} %stack.2), calls=%async_computation.1 | async-start | bytes 3145728 | tf_op jit(solution)/shard_map/all_to_all | solution.py:9
  14.5 3.4 %scatter_custom_fusion = bf16[256,2048]{1,0:T(8,128)(2,1)S(1)} fusion(s32[128]{0:T(128)S(1)} %fusion.21, bf16[16,2048]{1,0:T(8,128)(2,1)S(1)} %copy-done, s32[1024]{0:T(1024)S(1)} %pad_clamp_fusion.1, bf16[]{:T(256)} %constant.26.clone.1), kind=kCustom, calls=%fused_computation.27 | custom fusion | bytes 1048578 | tf_op jit(solution)/shard_map/scatter | solution.py:29
  19.3 14.1 %all-to-all-done.1 = bf16[4,1,512,384]{3,2,1,0:T(8,128)(2,1)S(1)} async-done(((bf16[4,1,512,384]{3,2,1,0:T(8,128)(2,1)}), bf16[4,1,512,384]{3,2,1,0:T(8,128)(2,1)S(1)}, u32[]{:S(2)}, u32[]{:S(2)}) %all-to-all-start.1) | async-done | bytes 1572896 | tf_op jit(solution)/shard_map/all_to_all | solution.py:9
  34.6 20.7 %all-to-all-start = ((bf16[128,2,2048]{2,1,0:T(2,128)(2,1)}), bf16[128,2,2048]{2,1,0:T(2,128)(2,1)S(1)}, u32[]{:S(2)}, u32[]{:S(2)}) async-start(bf16[128,2,2048]{2,1,0:T(2,128)(2,1)} %reshape.131), calls=%async_computation | async-start | bytes 2097152 | tf_op jit(solution)/shard_map/all_to_all | solution.py:40
  56.2 3.4 %scatter_custom_fusion.1 = bf16[256,2048]{1,0:T(8,128)(2,1)S(1)} fusion(s32[128]{0:T(128)S(1)} %fusion.21, f32[128]{0:T(128)S(1)} %mul.81, bf16[]{:T(256)} %constant.26.clone.1, bf16[16,2048]{1,0:T(8,128)(2,1)S(1)} %copy-done.7, s32[1024]{0:T(1024)S(1)} %pad_clamp_fusion.1), kind=kCustom, calls=%fused_computation.25 | custom fusion | flops 786432 | bytes 1118722 | tf_op jit(solution)/shard_map/scatter | solution.py:31
  59.6 1.5 reshape.135
  61.1 49.7 %all-to-all-done = bf16[128,2,2048]{2,1,0:T(2,128)(2,1)S(1)} async-done(((bf16[128,2,2048]{2,1,0:T(2,128)(2,1)}), bf16[128,2,2048]{2,1,0:T(2,128)(2,1)S(1)}, u32[]{:S(2)}, u32[]{:S(2)}) %all-to-all-start) | async-done | bytes 1048608 | tf_op jit(solution)/shard_map/all_to_all | solution.py:40
  110.9 6.4 %all-to-all-start.3 = ((bf16[128,2,2048]{2,1,0:T(2,128)(2,1)}), bf16[128,2,2048]{2,1,0:T(2,128)(2,1)S(1)}, u32[]{:S(2)}, u32[]{:S(2)}) async-start(bf16[128,2,2048]{2,1,0:T(2,128)(2,1)} %reshape.135), calls=%async_computation.3 | async-start | bytes 2097152 | tf_op jit(solution)/shard_map/all_to_all | solution.py:53
  118.6 2.9 fusion.4
  121.4 31.9 %all-gather.3.cloned.1.call-done = bf16[1,2048,384]{2,1,0:T(8,128)(2,1)} async-done(((bf16[1,512,384]{2,1,0:T(8,128)(2,1)}), bf16[1,2048,384]{2,1,0:T(8,128)(2,1)}) %all-gather.3.cloned.1.call-update) | async-done | bytes 1572880 | tf_op jit(solution)/shard_map/all_gather | solution.py:34
  153.4 2.3 fusion.8
  158.7 14.3 %all-to-all-done.3 = bf16[128,2,2048]{2,1,0:T(2,128)(2,1)S(1)} async-done(((bf16[128,2,2048]{2,1,0:T(2,128)(2,1)}), bf16[128,2,2048]{2,1,0:T(2,128)(2,1)S(1)}, u32[]{:S(2)}, u32[]{:S(2)}) %all-to-all-start.3) | async-done | bytes 1048608 | tf_op jit(solution)/shard_map/all_to_all | solution.py:53
  172.9 6.9 %all-to-all-start.2 = ((bf16[128,2,2048]{2,1,0:T(2,128)(2,1)}), bf16[128,2,2048]{2,1,0:T(2,128)(2,1)}, u32[]{:S(2)}, u32[]{:S(2)}) async-start(bf16[128,2,2048]{2,1,0:T(2,128)(2,1)} %reshape.133), calls=%async_computation.2 | async-start | bytes 2097152 | tf_op jit(solution)/shard_map/all_to_all | solution.py:52
  180.3 2.4 multiply_convert_fusion.2
  182.7 1.9 fusion
  188.3 46.8 %all-to-all-done.2 = bf16[128,2,2048]{2,1,0:T(2,128)(2,1)} async-done(((bf16[128,2,2048]{2,1,0:T(2,128)(2,1)}), bf16[128,2,2048]{2,1,0:T(2,128)(2,1)}, u32[]{:S(2)}, u32[]{:S(2)}) %all-to-all-start.2) | async-done | bytes 1048608 | tf_op jit(solution)/shard_map/all_to_all | solution.py:52
  235.1 6.4 %all-to-all-start.4 = ((bf16[128,2,2048]{2,1,0:T(2,128)(2,1)}), bf16[128,2,2048]{2,1,0:T(2,128)(2,1)S(1)}, u32[]{:S(2)}, u32[]{:S(2)}) async-start(bf16[128,2,2048]{2,1,0:T(2,128)(2,1)} %reshape.137), calls=%async_computation.4 | async-start | bytes 2097152 | tf_op jit(solution)/shard_map/all_to_all | solution.py:67
  241.8 1.9 fusion.1
  243.8 1.9 convert_element_type.76
  245.7 30.4 %reduce-scatter.5.cloned.1.call-done = bf16[1,512,384]{2,1,0:T(8,128)(2,1)} async-done(((bf16[1,2048,384]{2,1,0:T(8,128)(2,1)}), bf16[1,512,384]{2,1,0:T(8,128)(2,1)}) %reduce-scatter.5.cloned.1.call-update) | async-done | bytes 393232 | tf_op jit(solution)/shard_map/reduce_scatter | solution.py:75
  276.1 1.9 convert_element_type.79
  280.5 16.7 %all-to-all-done.4 = bf16[128,2,2048]{2,1,0:T(2,128)(2,1)S(1)} async-done(((bf16[128,2,2048]{2,1,0:T(2,128)(2,1)}), bf16[128,2,2048]{2,1,0:T(2,128)(2,1)S(1)}, u32[]{:S(2)}, u32[]{:S(2)}) %all-to-all-start.4) | async-done | bytes 1048608 | tf_op jit(solution)/shard_map/all_to_all | solution.py:67
  299.5 1.7 fusion.11
  (59 shorter events, 18.4 us)
Async XLA Ops:
  7.2 7.3 %copy-start = (bf16[16,2048]{1,0:T(8,128)(2,1)S(1)}, bf16[16,2048]{1,0:T(8,128)(2,1)}, u32[]{:S(2)}) copy-start(bf16[16,2048]{1,0:T(8,128)(2,1)} %param.7) | copy-start | bytes 196612
  9.5 4.1 %copy-start.8 = (s32[16,8]{0,1:T(8,128)S(1)}, s32[16,8]{0,1:T(8,128)}, u32[]{:S(2)}) copy-start(s32[16,8]{0,1:T(8,128)} %param.9) | copy-start | bytes 1540
  9.5 23.9 %all-to-all-start.1 = ((bf16[4,1,512,384]{3,2,1,0:T(8,128)(2,1)}), bf16[4,1,512,384]{3,2,1,0:T(8,128)(2,1)S(1)}, u32[]{:S(2)}, u32[]{:S(2)}) async-start(bf16[4,1,512,384]{3,2,1,0:T(8,128)(2,1)} %stack.2), calls=%async_computation.1 | async-start | bytes 3145728 | tf_op jit(solution)/shard_map/all_to_all | solution.py:9
  19.3 36.7 %copy-start.9 = (f32[16,8]{0,1:T(8,128)S(1)}, f32[16,8]{0,1:T(8,128)}, u32[]{:S(2)}) copy-start(f32[16,8]{0,1:T(8,128)} %param.10) | copy-start | bytes 1540
  19.3 36.9 %copy-start.7 = (bf16[16,2048]{1,0:T(8,128)(2,1)S(1)}, bf16[16,2048]{1,0:T(8,128)(2,1)}, u32[]{:S(2)}) copy-start(bf16[16,2048]{1,0:T(8,128)(2,1)} %param.8) | copy-start | bytes 196612
  33.4 1.1 copy-start.3
  34.6 76.3 %all-to-all-start = ((bf16[128,2,2048]{2,1,0:T(2,128)(2,1)}), bf16[128,2,2048]{2,1,0:T(2,128)(2,1)S(1)}, u32[]{:S(2)}, u32[]{:S(2)}) async-start(bf16[128,2,2048]{2,1,0:T(2,128)(2,1)} %reshape.131), calls=%async_computation | async-start | bytes 2097152 | tf_op jit(solution)/shard_map/all_to_all | solution.py:40
  55.3 63.3 %all-gather.5.cloned.1.call-start = ((), (), s32[]{:S(2)}) async-start(), calls=%async_computation.8 | async-start | bytes 1966080 | tf_op jit(solution)/shard_map/all_gather | solution.py:35
  110.9 62.1 %all-to-all-start.3 = ((bf16[128,2,2048]{2,1,0:T(2,128)(2,1)}), bf16[128,2,2048]{2,1,0:T(2,128)(2,1)S(1)}, u32[]{:S(2)}, u32[]{:S(2)}) async-start(bf16[128,2,2048]{2,1,0:T(2,128)(2,1)} %reshape.135), calls=%async_computation.3 | async-start | bytes 2097152 | tf_op jit(solution)/shard_map/all_to_all | solution.py:53
  117.3 36.0 %all-gather.3.cloned.1.call-start = ((), (), s32[]{:S(2)}) async-start(), calls=%async_computation.7 | async-start | bytes 1966080 | tf_op jit(solution)/shard_map/all_gather | solution.py:34
  153.4 3.0 copy-start.4
  153.4 3.0 copy-start.5
  155.6 0.7 copy-start.6
  172.9 62.2 %all-to-all-start.2 = ((bf16[128,2,2048]{2,1,0:T(2,128)(2,1)}), bf16[128,2,2048]{2,1,0:T(2,128)(2,1)}, u32[]{:S(2)}, u32[]{:S(2)}) async-start(bf16[128,2,2048]{2,1,0:T(2,128)(2,1)} %reshape.133), calls=%async_computation.2 | async-start | bytes 2097152 | tf_op jit(solution)/shard_map/all_to_all | solution.py:52
  179.8 63.9 %reduce-scatter.3.cloned.1.call-start = ((), (), s32[]{:S(2)}) async-start(), calls=%async_computation.9 | async-start | bytes 1966080 | tf_op jit(solution)/shard_map/reduce_scatter | solution.py:72
  182.7 1.9 copy-start.2
  184.6 1.4 copy-start.1
  235.1 62.1 %all-to-all-start.4 = ((bf16[128,2,2048]{2,1,0:T(2,128)(2,1)}), bf16[128,2,2048]{2,1,0:T(2,128)(2,1)S(1)}, u32[]{:S(2)}, u32[]{:S(2)}) async-start(bf16[128,2,2048]{2,1,0:T(2,128)(2,1)} %reshape.137), calls=%async_computation.4 | async-start | bytes 2097152 | tf_op jit(solution)/shard_map/all_to_all | solution.py:67
  241.6 34.6 %reduce-scatter.5.cloned.1.call-start = ((), (), s32[]{:S(2)}) async-start(), calls=%async_computation.10 | async-start | bytes 1966080 | tf_op jit(solution)/shard_map/reduce_scatter | solution.py:75
Sparse Core Ops, SparseCore 0:
  58.2 33.0 all-gather.4
  120.3 33.0 all-gather.2
  184.8 31.1 reduce-scatter.2
  244.9 31.1 reduce-scatter.4
